TPU v7x, 128 devices: a whole 4x4x4 slice. The times are simulated.
128 devices in a mesh: region: 8 (over x, core), cols: 16 (over y, z).
Axes of the slice: x: 4, y: 4, z: 4, core: 2. Of those that a mesh axis runs over, the one named last changes fastest.
Arguments:
- ensemble: float32 [80, 524288], P('cols', 'region'), may hold values from -6 to 6
- obs_value: float32 [64], replicated, may hold values from -6 to 6
- obs_error: float32 [64], replicated, may hold values from 0.25 to 2
- observation_holder: int32 [64], replicated, may hold values from 0 to 127
- obs_column: int32 [64], replicated, may hold values from 0 to 4095
- loc_mask: int32 [64, 8], replicated, may hold values 0 or 1
- loc_taper: float32 [64, 8], replicated, may hold values from 0.2 to 1
Outputs:
- analysis: float32 [80, 524288], P('cols', 'region')
All inputs are finite; a program needn't handle non-finite values.
Results may differ from a plain program's by a relative error of at most 0.0003.
Values sent between devices are 32-bit elements; how exact they have to be, the bound alone decides.
No kernel may reach another device: no remote copies, remote signals or barrier semaphores. Data moves between devices by JAX's collectives and lax.ppermute only.
A program may use at most 128 MiB of HBM per device.

v0:
```python
import jax
import jax.numpy as jnp
from jax import lax
from jax.sharding import PartitionSpec as P

NB = 16
BATCHES = 4


highest = lax.Precision.HIGHEST


def assimilate(block, update_transforms, index, value, error, mutual_row, weight_row):
    member_list = block.shape[0]
    prior = lax.dynamic_index_in_dim(block, index, 1, keepdims=False)
    center = jnp.mean(prior)
    spread = prior - center
    variance = jnp.sum(spread * spread) / (member_list - 1)
    summed = variance + error
    scaling = 1.0 / ((member_list - 1) * summed)
    reduction = 1.0 / (1.0 + jnp.sqrt(error / summed))
    shift = value - center - reduction * spread
    later = (jnp.arange(block.shape[1], dtype=jnp.int32) > index).astype(jnp.float32)
    factor = jnp.dot(spread, block, precision=highest) * mutual_row * later * scaling
    block = block + shift[:, None] * factor[None, :]
    project = jnp.einsum("m,rmn->rn", spread, update_transforms, precision=highest)
    update_transforms = (
        update_transforms
        + (weight_row * scaling)[:, None, None] * shift[None, :, None] * project[:, None, :]
    )
    return (block, update_transforms)


def run_chain(block, update_transforms, base, offset, count, obs_value, obs_error, mutual, weight):
    width = block.shape[1]

    def turn(step, carry):
        current, region_local = carry
        member_count = offset + step
        mutual_row = lax.dynamic_index_in_dim(mutual, member_count, 0, keepdims=False)[
            base : base + width
        ]
        return assimilate(
            current,
            region_local,
            member_count - base,
            obs_value[member_count],
            obs_error[member_count],
            mutual_row,
            weight[member_count],
        )

    return lax.fori_loop(0, count, turn, (block, update_transforms))


def per_device(ensemble, obs_value, obs_error, observation_holder, obs_column, loc_mask, loc_taper):
    ncols = lax.axis_size("cols")
    nregion = lax.axis_size("region")
    region_index = lax.axis_index("region")
    block_index = lax.axis_index("cols")
    members_dev = ensemble.shape[0]
    member_list = members_dev * ncols
    weight = loc_mask.astype(jnp.float32) * loc_taper
    home = observation_holder // ncols
    onehot = (home[:, None] == jnp.arange(nregion, dtype=jnp.int32)[None, :]).astype(jnp.float32)
    mutual = jnp.dot(weight, onehot.T, precision=highest)
    identity = jnp.broadcast_to(
        jnp.eye(member_list, dtype=jnp.float32), (nregion, member_list, member_list)
    )
    device = region_index * ncols + block_index
    state = lax.all_to_all(ensemble, "cols", split_axis=1, concat_axis=0, tiled=True)
    for batch in range(BATCHES):
        lower = batch * NB
        owners = observation_holder[lower : lower + NB]
        columns = obs_column[lower : lower + NB]
        owned = (owners == device).astype(jnp.float32)
        priors = lax.psum(jnp.take(state, columns, axis=1) * owned[None, :], ("region", "cols"))
        unused, update_transforms = run_chain(
            priors, identity, lower, lower, NB, obs_value, obs_error, mutual, weight
        )
        local_batch = lax.dynamic_index_in_dim(update_transforms, region_index, 0, keepdims=False)
        state = jnp.dot(local_batch, state, precision=highest)
    return lax.all_to_all(state, "cols", split_axis=0, concat_axis=1, tiled=True)


def solution(mesh):
    placed = (P("cols", "region"), P(), P(), P(), P(), P(), P())
    return jax.shard_map(
        per_device, mesh=mesh, in_specs=placed, out_specs=P("cols", "region"), check_vma=False
    )
```

profile of v0, /device:TPU:0, one launch (start us, length us, event | category | flops | bytes accessed | tf_op | source)
XLA Modules:
  0.0 786.3 jit_solution(14129773580266500885)
XLA Ops:
  0.0 8.3 %all-to-all-start = ((f32[5,16,4096]{2,0,1:T(8,128)}), f32[5,16,4096]{2,0,1:T(8,128)S(1)}, u32[]{:S(2)}, u32[]{:S(2)}) async-start(f32[5,16,4096]{2,0,1:T(8,128)} %bitcast.263), calls=%async_computation | async-start | bytes 4194304 | tf_op jit(solution)/shard_map/all_to_all | solution.py:71
  9.5 29.2 %all-to-all-done = f32[5,16,4096]{2,0,1:T(8,128)S(1)} async-done(((f32[5,16,4096]{2,0,1:T(8,128)}), f32[5,16,4096]{2,0,1:T(8,128)S(1)}, u32[]{:S(2)}, u32[]{:S(2)}) %all-to-all-start) | async-done | bytes 1310752 | tf_op jit(solution)/shard_map/all_to_all | solution.py:71
  40.0 1.8 all_to_all.29
  41.9 1.8 copy.23
  43.6 2.2 gather_fusion
  45.9 62.7 %psum.28 = f32[80,16]{0,1:T(8,128)S(1)} all-reduce(f32[80,16]{0,1:T(8,128)S(1)} %bitcast_multiply_fusion.11), channel_id=1, replica_groups=mesh['region'=8,'cols'=16] {'region','cols'}, use_global_device_ids=true, to_apply=%region_0.2 | all-reduce | flops 1280 | bytes 10240 | tf_op jit(solution)/shard_map/psum | solution.py:77
  108.6 105.4 %while.72 = (s32[]{:T(128)}, f32[80,16]{0,1:T(8,128)S(1)}, f32[8,80,80]{2,1,0:T(8,128)S(1)}, f32[64]{0:T(128)S(1)}, f32[64]{0:T(128)S(1)}, /*index=5*/f32[64,64]...) while((s32[]{:T(128)}, f32[80,16]{0,1:T(8,128)S(1)}, ...), condition=%wide.region_4.6_spmd, body=%wide.region_1.5_spmd.sunk | while | flops 736081 | bytes 644633 | solution.py:53
  217.4 64.3 %psum.29 = f32[80,16]{0,1:T(8,128)S(1)} all-reduce(f32[80,16]{0,1:T(8,128)S(1)} %bitcast_multiply_fusion.10), channel_id=1, replica_groups=mesh['region'=8,'cols'=16] {'region','cols'}, use_global_device_ids=true, to_apply=%region_5.7 | all-reduce | flops 1280 | bytes 10240 | tf_op jit(solution)/shard_map/psum | solution.py:77
  281.7 126.7 %while.73 = (s32[]{:T(128)}, f32[80,16]{0,1:T(8,128)S(1)}, f32[8,80,80]{2,1,0:T(8,128)S(1)}, f32[64]{0:T(128)}, f32[64]{0:T(128)}, /*index=5*/f32[64,64]{1,0:T(8...) while((s32[]{:T(128)}, f32[80,16]{0,1:T(8,128)S(1)}, ...), condition=%wide.region_9.11_spmd, body=%wide.region_6.10_spmd.sunk | while | flops 736085 | bytes 644703 | solution.py:53
  289.7 1.3 dynamic_slice.338
  313.4 1.3 dynamic_slice.338
  337.2 1.3 dynamic_slice.338
  345.1 1.3 dynamic_slice.338
  360.9 1.3 dynamic_slice.338
  368.9 1.3 dynamic_slice.338
  392.6 1.3 dynamic_slice.338
  409.8 1.8 copy.27
  411.5 2.2 gather_fusion.2
  413.8 62.3 %psum.30 = f32[80,16]{0,1:T(8,128)S(1)} all-reduce(f32[80,16]{0,1:T(8,128)S(1)} %bitcast_multiply_fusion.9), channel_id=1, replica_groups=mesh['region'=8,'cols'=16] {'region','cols'}, use_global_device_ids=true, to_apply=%region_10.12 | all-reduce | flops 1280 | bytes 10240 | tf_op jit(solution)/shard_map/psum | solution.py:77
  476.1 105.3 %while.74 = (s32[]{:T(128)}, f32[80,16]{0,1:T(8,128)S(1)}, f32[8,80,80]{2,1,0:T(8,128)S(1)}, f32[64]{0:T(128)S(1)}, f32[64]{0:T(128)S(1)}, /*index=5*/f32[64,64]...) while((s32[]{:T(128)}, f32[80,16]{0,1:T(8,128)S(1)}, ...), condition=%wide.region_14.16_spmd, body=%wide.region_11.15_spmd.sunk | while | flops 736085 | bytes 644703 | solution.py:53
  584.1 64.8 %psum.31 = f32[80,16]{0,1:T(8,128)S(1)} all-reduce(f32[80,16]{0,1:T(8,128)S(1)} %bitcast_multiply_fusion.8), channel_id=1, replica_groups=mesh['region'=8,'cols'=16] {'region','cols'}, use_global_device_ids=true, to_apply=%region_15.17 | all-reduce | flops 1280 | bytes 10240 | tf_op jit(solution)/shard_map/psum | solution.py:77
  648.9 102.3 %while.75 = (s32[]{:T(128)}, f32[80,16]{0,1:T(8,128)S(1)}, f32[8,80,80]{2,1,0:T(8,128)S(1)}, f32[64]{0:T(128)S(1)}, f32[64]{0:T(128)S(1)}, /*index=5*/f32[64,64]...) while((s32[]{:T(128)}, f32[80,16]{0,1:T(8,128)S(1)}, ...), condition=%wide.region_19.21_spmd, body=%wide.region_16.20_spmd.sunk | while | flops 736085 | bytes 644703 | solution.py:53
  753.4 31.6 %all_to_all.35 = f32[16,5,4096]{2,1,0:T(8,128)S(1)} all-to-all(f32[16,5,4096]{2,1,0:T(8,128)S(1)} %copy.30), channel_id=1, replica_groups=mesh['region'=8,'cols'=16] {'cols'}, dimensions={0} | all-to-all | bytes 2621440 | tf_op jit(solution)/shard_map/all_to_all | solution.py:83
  785.0 1.3 copy.77
  (874 shorter events, 227.3 us)
Async XLA Ops:
  0.0 8.3 %copy-start.4 = (s32[64,8]{0,1:T(8,128)S(1)}, s32[64,8]{0,1:T(8,128)}, u32[]{:S(2)}) copy-start(s32[64,8]{0,1:T(8,128)} %param.22) | copy-start | bytes 6148
  0.0 8.4 %copy-start.3 = (f32[64,8]{0,1:T(8,128)S(1)}, f32[64,8]{0,1:T(8,128)}, u32[]{:S(2)}) copy-start(f32[64,8]{0,1:T(8,128)} %param.23) | copy-start | bytes 6148
  0.0 8.5 %copy-start.1 = (s32[64]{0:T(128)S(1)}, s32[64]{0:T(128)}, u32[]{:S(2)}) copy-start(s32[64]{0:T(128)} %param.21) | copy-start | bytes 772
  0.0 8.5 %copy-start.2 = (s32[64]{0:T(128)S(1)}, s32[64]{0:T(128)}, u32[]{:S(2)}) copy-start(s32[64]{0:T(128)} %param.20) | copy-start | bytes 772
  0.0 38.7 %all-to-all-start = ((f32[5,16,4096]{2,0,1:T(8,128)}), f32[5,16,4096]{2,0,1:T(8,128)S(1)}, u32[]{:S(2)}, u32[]{:S(2)}) async-start(f32[5,16,4096]{2,0,1:T(8,128)} %bitcast.263), calls=%async_computation | async-start | bytes 4194304 | tf_op jit(solution)/shard_map/all_to_all | solution.py:71
  38.7 1.3 copy-start
  41.8 66.7 %copy-start.5 = (f32[64]{0:T(128)S(1)}, f32[64]{0:T(128)}, u32[]{:S(2)}) copy-start(f32[64]{0:T(128)} %param.18) | copy-start | bytes 772
  41.8 66.7 %copy-start.7 = (f32[64]{0:T(128)S(1)}, f32[64]{0:T(128)}, u32[]{:S(2)}) copy-start(f32[64]{0:T(128)} %param.19) | copy-start | bytes 772
  409.7 66.3 %copy-start.6 = (f32[64]{0:T(128)S(1)}, f32[64]{0:T(128)}, u32[]{:S(2)}) copy-start(f32[64]{0:T(128)} %get-tuple-element.1276) | copy-start | bytes 772
  409.8 66.3 %copy-start.8 = (f32[64]{0:T(128)S(1)}, f32[64]{0:T(128)}, u32[]{:S(2)}) copy-start(f32[64]{0:T(128)} %get-tuple-element.1279) | copy-start | bytes 772
where the time goes:
time: 790 us; the launch traced here: 786 us
  blocking collectives  286 us (36%)
  loops' own time  215 us (27%)
  local copies, waits for them, and re-layouts  115 us (15%)
  other arithmetic  104 us (13%)
  waiting for transfers between devices  29.2 us (4%)
  matrix products  28.3 us (4%)
  starting transfers between devices  8.29 us (1%)
    psum x4, blocking collectives, per_device(): lax.psum(jnp.take(state, columns, axis=1) * owned[None, :], ('region', 'c...  254 us
    another operation x4, loops' own time, run_chain(): return lax.fori_loop(0, count, turn, (block, update_transforms))  215 us
    dynamic_slice x64, local copies, waits for them, and re-layouts, turn(): obs_error[member_count]  49.9 us
    dynamic_slice x64, local copies, waits for them, and re-layouts, turn(): obs_value[member_count]  48.2 us
    reduce_sum x64, other arithmetic, assimilate(): variance = jnp.sum(spread * spread) / (member_list - 1)  39.1 us
    reduce_sum x64, other arithmetic, assimilate(): center = jnp.mean(prior)  38.8 us
    all_to_all x1, blocking collectives, per_device(): lax.all_to_all(state, 'cols', split_axis=0, concat_axis=1, tiled=True)  31.6 us
    all_to_all x1, waiting for transfers between devices, per_device(): lax.all_to_all(ensemble, 'cols', split_axis=1, concat_axis=0, tiled=True)  29.2 us
  transfers between devices with their start and end apart: 1, of which 1 were waited for; matrix products, arithmetic and copies ran while one was open for 0% of the time, Pallas kernels for 0%

commit v1 on v0

v1 whole, which is shorter than its diff:
```python
import jax
import jax.numpy as jnp
from jax import lax
from jax.experimental import pallas as pl
from jax.experimental.pallas import tpu as pltpu
from jax.sharding import PartitionSpec as P

MEMBERS = 80
NOBS = 64
COLS = 16
REGIONS = 8
OWN = 5
S_DEV = 4096
REGION_COLUMNS = COLS * S_DEV
PIECE = 512
HEAD = OWN * PIECE
TAILS = 3
PADDED = COLS * 8
GROUP = 4
BLOCK = 4

highest = lax.Precision.HIGHEST
SMEM = pl.BlockSpec(memory_space=pltpu.SMEM)
VMEM = pl.BlockSpec(memory_space=pltpu.VMEM)


def params(**more):
    return pltpu.CompilerParams(vmem_limit_bytes=40 << 20, **more)


def split_kernel(where_ref, mine_ref, block_ref, whole_ref, packed_ref, sent_ref, tiles, sems):
    step = pl.program_id(0)

    def fetch(k):
        start = pl.multiple_of((where_ref[k] // 128) * 128, 128)
        return pltpu.make_async_copy(whole_ref.at[:, pl.ds(start, 128)], tiles.at[k], sems.at[k])

    @pl.when(step == 0)
    def _():
        for k in range(NOBS):
            fetch(k).start()

    for b in range(GROUP):
        low = b * S_DEV
        packed_ref[b, 0:OWN, :] = block_ref[:, low : low + HEAD]
        for i in range(TAILS):
            for q in range(OWN):
                at = low + HEAD + i * PIECE
                packed_ref[b, OWN + i : OWN + i + 1, q * PIECE : (q + 1) * PIECE] = block_ref[
                    q : q + 1, at : at + PIECE
                ]

    @pl.when(step == pl.num_programs(0) - 1)
    def _():
        lane = lax.broadcasted_iota(jnp.int32, (OWN, 128), 1)
        got = jnp.zeros((OWN, 128), jnp.float32)
        for k in range(NOBS):
            fetch(k).wait()
            turned = pltpu.roll(tiles[k], lax.rem(k + 128 - lax.rem(where_ref[k], 128), 128), 1)
            got = jnp.where(lane == jnp.where(mine_ref[k] == 1, k, -1), turned, got)
        full = jnp.concatenate([got, jnp.zeros((8 - OWN, 128), jnp.float32)], axis=0)
        sent_ref[...] = jnp.broadcast_to(full[None], sent_ref.shape)


def split(where, mine, ensemble):
    return pl.pallas_call(
        split_kernel,
        grid=(COLS // GROUP,),
        in_specs=[
            SMEM,
            SMEM,
            pl.BlockSpec((OWN, GROUP * S_DEV), lambda s: (0, s)),
            pl.BlockSpec(memory_space=pl.ANY),
        ],
        out_specs=[
            pl.BlockSpec((GROUP, 8, HEAD), lambda s: (s, 0, 0)),
            pl.BlockSpec((REGIONS * COLS, 8, 128), lambda s: (0, 0, 0)),
        ],
        out_shape=[
            jax.ShapeDtypeStruct((COLS, 8, HEAD), jnp.float32),
            jax.ShapeDtypeStruct((REGIONS * COLS, 8, 128), jnp.float32),
        ],
        scratch_shapes=[
            pltpu.VMEM((NOBS, OWN, 128), jnp.float32),
            pltpu.SemaphoreType.DMA((NOBS,)),
        ],
        compiler_params=params(),
        name="split",
    )(where, mine, ensemble, ensemble)


def total(x):
    return jnp.sum(x, axis=0, keepdims=True)


def chain_kernel(value_ref, error_ref, own_ref, got_ref, weight_ref, out_ref, scratch):
    gathered = got_ref[0:COLS]
    for r in range(1, REGIONS):
        gathered = gathered + got_ref[r * COLS : (r + 1) * COLS]
    for c in range(COLS):
        scratch[OWN * c : OWN * (c + 1), :] = gathered[c, 0:OWN, :]
    priors = scratch[...]
    mean = total(priors) * (1.0 / MEMBERS)
    spread = priors - mean
    row = lax.broadcasted_iota(jnp.int32, (MEMBERS, 128), 0)
    lane = lax.broadcasted_iota(jnp.int32, (MEMBERS, 128), 1)
    turn = ((row // OWN) * 8 + lax.rem(row, OWN) == lane).astype(jnp.float32)
    lift = jnp.zeros((1, 128), jnp.float32)
    for low in range(0, NOBS, BLOCK):
        near = range(low, low + BLOCK)
        ps = {k: jnp.broadcast_to(spread[:, k : k + 1], (MEMBERS, 128)) for k in near}
        ms = {k: jnp.broadcast_to(mean[:, k : k + 1], (1, 128)) for k in near}
        for j in near:
            p = ps[j]
            e = error_ref[j]
            s = total(p * p) * (1.0 / (MEMBERS - 1)) + e
            scaling = 1.0 / ((MEMBERS - 1) * s)
            damped = 1.0 / ((MEMBERS - 1) * (s + jnp.sqrt(e * s)))
            move = (value_ref[j] - ms[j]) * scaling
            for k in range(j + 1, low + BLOCK):
                w = jnp.broadcast_to(weight_ref[j : j + 1, k : k + 1], (1, 128))
                f = w * total(p * ps[k])
                ps[k] = ps[k] - p * (f * damped)
                ms[k] = ms[k] + move * f
            f = weight_ref[j : j + 1, :] * total(p * spread)
            h = own_ref[j] * total(p * turn)
            spread = spread - p * (f * damped)
            turn = turn - p * (h * damped)
            mean = mean + move * f
            lift = lift + move * h
    turn = turn + lift
    for c in range(COLS):
        out_ref[8 * c : 8 * c + OWN, :] = turn[OWN * c : OWN * (c + 1), :]
        out_ref[8 * c + OWN : 8 * (c + 1), :] = jnp.zeros((8 - OWN, 128), jnp.float32)


def chain(value, error, own, got, weight):
    return pl.pallas_call(
        chain_kernel,
        in_specs=[SMEM, SMEM, SMEM, VMEM, VMEM],
        out_specs=VMEM,
        out_shape=jax.ShapeDtypeStruct((PADDED, 128), jnp.float32),
        scratch_shapes=[pltpu.VMEM((MEMBERS, 128), jnp.float32)],
        compiler_params=params(),
        cost_estimate=pl.CostEstimate(flops=20_000_000, bytes_accessed=20_000_000, transcendentals=0),
        name="chain",
    )(value, error, own, got, weight)


def apply_kernel(turn_ref, got_ref, out_ref, tail):
    turn = turn_ref[...]
    for q in range(OWN):
        span = slice(q * PIECE, (q + 1) * PIECE)
        x = got_ref[:, :, span].reshape(PADDED, PIECE)
        y = jnp.dot(turn, x, precision=highest, preferred_element_type=jnp.float32)
        out_ref[:, 0:OWN, span] = y.reshape(COLS, 8, PIECE)[:, 0:OWN]
    for i in range(TAILS):
        tail[...] = jnp.zeros_like(tail)
        for q in range(OWN):
            for c in range(COLS):
                tail[8 * c + q : 8 * c + q + 1, :] = got_ref[
                    c, OWN + i : OWN + i + 1, q * PIECE : (q + 1) * PIECE
                ]
        y = jnp.dot(turn, tail[...], precision=highest, preferred_element_type=jnp.float32)
        for q in range(OWN):
            for c in range(COLS):
                out_ref[c, OWN + i : OWN + i + 1, q * PIECE : (q + 1) * PIECE] = y[
                    8 * c + q : 8 * c + q + 1, :
                ]


def apply(turn, got):
    return pl.pallas_call(
        apply_kernel,
        in_specs=[VMEM, VMEM],
        out_specs=VMEM,
        out_shape=jax.ShapeDtypeStruct((COLS, 8, HEAD), jnp.float32),
        scratch_shapes=[pltpu.VMEM((PADDED, PIECE), jnp.float32)],
        compiler_params=params(),
        name="apply",
    )(turn, got)


def join_kernel(packed_ref, out_ref):
    for b in range(GROUP):
        low = b * S_DEV
        out_ref[:, low : low + HEAD] = packed_ref[b, 0:OWN, :]
        for i in range(TAILS):
            for q in range(OWN):
                at = low + HEAD + i * PIECE
                out_ref[q : q + 1, at : at + PIECE] = packed_ref[
                    b, OWN + i : OWN + i + 1, q * PIECE : (q + 1) * PIECE
                ]


def join(packed):
    return pl.pallas_call(
        join_kernel,
        grid=(COLS // GROUP,),
        in_specs=[pl.BlockSpec((GROUP, 8, HEAD), lambda s: (s, 0, 0))],
        out_specs=pl.BlockSpec((OWN, GROUP * S_DEV), lambda s: (0, s)),
        out_shape=jax.ShapeDtypeStruct((OWN, REGION_COLUMNS), jnp.float32),
        compiler_params=params(),
        name="join",
    )(packed)


def per_device(ensemble, obs_value, obs_error, observation_holder, obs_column, loc_mask, loc_taper):
    region = lax.axis_index("region")
    weight = loc_mask.astype(jnp.float32) * loc_taper
    home = observation_holder // COLS
    mine = (home == region).astype(jnp.int32)
    where = (observation_holder - home * COLS) * S_DEV + obs_column
    mutual = jnp.zeros((NOBS, NOBS), jnp.float32)
    for r in range(REGIONS):
        mutual = jnp.where(home[None, :] == r, weight[:, r : r + 1], mutual)
    mutual = jnp.pad(mutual, ((0, 0), (0, 128 - NOBS)))
    own = lax.dynamic_index_in_dim(weight, region, 1, keepdims=False)
    packed, sent = split(where, mine, ensemble)
    state = lax.all_to_all(packed, "cols", 0, 0)
    got = lax.all_to_all(sent, ("region", "cols"), 0, 0)
    turn = chain(obs_value, obs_error, own, got, mutual)
    state = apply(turn, state)
    state = lax.all_to_all(state, "cols", 0, 0)
    return join(state)


def solution(mesh):
    placed = (P("cols", "region"), P(), P(), P(), P(), P(), P())
    return jax.shard_map(
        per_device, mesh=mesh, in_specs=placed, out_specs=P("cols", "region"), check_vma=False
    )
```

time: 790 us -> 86.4 us (0.11)
  blocking collectives: 286 us -> 46.4 us
  loops' own time: 215 us -> 0 us
  local copies, waits for them, and re-layouts: 115 us -> 1.62 us
  other arithmetic: 104 us -> 1.49 us
  matrix products: 28.3 us -> 0 us
  Pallas kernels: 0 us -> 16.7 us
  waiting for transfers between devices: 29.2 us -> 16 us
    psum x4 -> x0, blocking collectives: 254 us -> none  [per_device(): lax.psum(jnp.take(state, columns, axis=1) * owned[None, :], ('region', 'c...]
    another operation x4 -> x0, loops' own time: 215 us -> none  [run_chain(): return lax.fori_loop(0, count, turn, (block, update_transforms))]
    dynamic_slice x193 -> x0, local copies, waits for them, and re-layouts: 98.9 us -> none  [the longest x64 49.9 us: turn(): obs_error[member_count]]
    reduce_sum x128 -> x0, other arithmetic: 77.9 us -> none  [the longest x64 39.1 us: assimilate(): variance = jnp.sum(spread * spread) / (member_list - 1)]
    dot_general x133 -> x0, matrix products: 28.3 us -> none  [the longest x64 17.2 us: assimilate(): jnp.einsum('m,rmn->rn', spread, update_transforms, precision=highest)]
    add x128 -> x1, other arithmetic: 18.5 us -> 0.68 us  [per_device(): where = (observation_holder - home * COLS) * S_DEV + obs_column]
    pallas_call x0 -> x4, Pallas kernels: none -> 16.7 us  [the longest x1 8.07 us: split(): pl.pallas_call(split_kernel, grid=(COLS // GROUP,), in_specs=[SMEM, SMEM,...]
    all_to_all x1 -> x2, blocking collectives: 31.6 us -> 46.4 us  [the longest x1 24.6 us: per_device(): got = lax.all_to_all(sent, ('region', 'cols'), 0, 0)]
  transfers between devices with their start and end apart: 1 -> 1, of which waited for: 1 -> 1; matrix products, arithmetic and copies ran while one was open for 0% -> 0% of each run, Pallas kernels for 0% -> 5%
where the time goes in v1:
time: 86.4 us; the launch traced here: 86.1 us
  blocking collectives  46.4 us (54%)
  Pallas kernels  16.7 us (19%)
  waiting for transfers between devices  16 us (19%)
  starting transfers between devices  3.85 us (4%)
  local copies, waits for them, and re-layouts  1.62 us (2%)
  other arithmetic  1.49 us (2%)
    all_to_all x1, blocking collectives, per_device(): got = lax.all_to_all(sent, ('region', 'cols'), 0, 0)  24.6 us
    all_to_all x1, blocking collectives, per_device(): state = lax.all_to_all(state, 'cols', 0, 0)  21.8 us
    all_to_all x1, waiting for transfers between devices, per_device(): state = lax.all_to_all(packed, 'cols', 0, 0)  16 us
    pallas_call x1, Pallas kernels, split(): pl.pallas_call(split_kernel, grid=(COLS // GROUP,), in_specs=[SMEM, SMEM,...  8.07 us
    pallas_call x1, Pallas kernels, chain(): pl.pallas_call(chain_kernel, in_specs=[SMEM, SMEM, SMEM, VMEM, VMEM], out...  4.7 us
    all_to_all x1, starting transfers between devices, per_device(): state = lax.all_to_all(packed, 'cols', 0, 0)  3.85 us
    pallas_call x1, Pallas kernels, apply(): pl.pallas_call(apply_kernel, in_specs=[VMEM, VMEM], out_specs=VMEM, out_s...  2 us
    pallas_call x1, Pallas kernels, join(): pl.pallas_call(join_kernel, grid=(COLS // GROUP,), in_specs=[pl.BlockSpec...  1.88 us
  transfers between devices with their start and end apart: 1, of which 1 were waited for; matrix products, arithmetic and copies ran while one was open for 0% of the time, Pallas kernels for 5%

profile of v1, /device:TPU:0, one launch (start us, length us, event | category | flops | bytes accessed | tf_op | source)
XLA Modules:
  0.0 86.1 jit_solution(7858073878961123837)
XLA Ops:
  0.0 0.7 broadcast_compare_fusion.4
  0.7 0.7 multiply_add_fusion.where_ref
  1.4 0.0 copy-start
  1.4 1.6 %copy-done = f32[5,65536]{1,0:T(8,128)S(1)} copy-done((f32[5,65536]{1,0:T(8,128)S(1)}, f32[5,65536]{1,0:T(8,128)}, u32[]{:S(2)}) %copy-start) | copy-done | bytes 1310744
  3.0 8.1 %split.1 = (f32[16,8,2560]{2,1,0:T(8,128)}, f32[128,8,128]{2,1,0:T(8,128)S(1)}) custom-call(s32[64]{0:T(128)S(1)} %multiply_add_fusion.where_ref, s32[64]{0:T(128)S(1)} %get-tuple-element.27.mine_ref, f32[5,65536]{1,0:T(8,128)S(1)} %copy-done, f32[5,65536]{1,0:T(8,128)S(1)} %copy-done), custom_call_target="tpu_custom_call" | custom-call | tf_op jit(solution)/shard_map/split/pallas_call | solution.py:66
  11.0 24.6 %all_to_all.15.got_ref = f32[128,8,128]{2,1,0:T(8,128)S(1)} all-to-all(f32[128,8,128]{2,1,0:T(8,128)S(1)} %get-tuple-element.7), channel_id=1, replica_groups=mesh['region'=8,'cols'=16] {'region','cols'}, dimensions={0} | all-to-all | bytes 1048576 | tf_op jit(solution)/shard_map/all_to_all | solution.py:221
  35.6 0.0 copy-start.3
  35.6 0.0 copy-start.4
  35.6 0.0 copy-start.1
  35.6 0.0 copy-start.2
  35.6 3.8 %all-to-all-start.1 = ((f32[16,8,2560]{2,1,0:T(8,128)}), f32[16,8,2560]{2,1,0:T(8,128)S(1)}, u32[]{:S(2)}, u32[]{:S(2)}) async-start(f32[16,8,2560]{2,1,0:T(8,128)} %get-tuple-element.8), calls=%async_computation.1 | async-start | bytes 2621440 | tf_op jit(solution)/shard_map/all_to_all | solution.py:220
  39.5 0.0 copy-done.3
  39.5 0.0 copy-done.4
  39.5 0.1 select_select_fusion
  39.7 0.0 copy-done.1
  39.7 0.0 copy-done.2
  39.7 4.7 %chain.1.turn_ref = f32[128,128]{1,0:T(8,128)S(1)} custom-call(f32[64]{0:T(128)S(1)} %copy-done.1, f32[64]{0:T(128)S(1)} %copy-done.2, f32[64]{0:T(128)S(1)} %get-tuple-element.19.own_ref, f32[128,8,128]{2,1,0:T(8,128)S(1)} %all_to_all.15.got_ref, f32[64,128]{1,0:T(8,128)S(1)} %pad.4.weight_ref), custom_call_target="tpu_custom_call" | custom-call | flops 20000000 | bytes 20000000 | tf_op jit(solution)/shard_map/chain/pallas_call | solution.py:138
  44.4 16.0 %all-to-all-done.1.got_ref = f32[16,8,2560]{2,1,0:T(8,128)S(1)} async-done(((f32[16,8,2560]{2,1,0:T(8,128)}), f32[16,8,2560]{2,1,0:T(8,128)S(1)}, u32[]{:S(2)}, u32[]{:S(2)}) %all-to-all-start.1) | async-done | bytes 1310752 | tf_op jit(solution)/shard_map/all_to_all | solution.py:220
  60.4 2.0 %apply.1 = f32[16,8,2560]{2,1,0:T(8,128)S(1)} custom-call(f32[128,128]{1,0:T(8,128)S(1)} %chain.1.turn_ref, f32[16,8,2560]{2,1,0:T(8,128)S(1)} %all-to-all-done.1.got_ref), custom_call_target="tpu_custom_call" | custom-call | tf_op jit(solution)/shard_map/apply/pallas_call | solution.py:173
  62.4 21.8 %all_to_all.16.packed_ref = f32[16,8,2560]{2,1,0:T(8,128)S(1)} all-to-all(f32[16,8,2560]{2,1,0:T(8,128)S(1)} %apply.1), channel_id=1, replica_groups=mesh['region'=8,'cols'=16] {'cols'}, dimensions={0} | all-to-all | bytes 2621440 | tf_op jit(solution)/shard_map/all_to_all | solution.py:224
  84.2 1.9 %join.1 = f32[5,65536]{1,0:T(8,128)} custom-call(f32[16,8,2560]{2,1,0:T(8,128)S(1)} %all_to_all.16.packed_ref), custom_call_target="tpu_custom_call" | custom-call | tf_op jit(solution)/shard_map/join/pallas_call | solution.py:197
  (4 shorter events, 0.0 us)
Async XLA Ops:
  1.4 1.6 %copy-start = (f32[5,65536]{1,0:T(8,128)S(1)}, f32[5,65536]{1,0:T(8,128)}, u32[]{:S(2)}) copy-start(f32[5,65536]{1,0:T(8,128)} %whole_ref.1) | copy-start | bytes 3932164
  35.6 3.9 %copy-start.3 = (f32[64,8]{0,1:T(8,128)S(1)}, f32[64,8]{0,1:T(8,128)}, u32[]{:S(2)}) copy-start(f32[64,8]{0,1:T(8,128)} %param.13) | copy-start | bytes 6148
  35.6 3.9 %copy-start.4 = (s32[64,8]{0,1:T(8,128)S(1)}, s32[64,8]{0,1:T(8,128)}, u32[]{:S(2)}) copy-start(s32[64,8]{0,1:T(8,128)} %param.12) | copy-start | bytes 6148
  35.6 4.1 %copy-start.1 = (f32[64]{0:T(128)S(1)}, f32[64]{0:T(128)}, u32[]{:S(2)}) copy-start(f32[64]{0:T(128)} %value_ref.1) | copy-start | bytes 772
  35.6 4.1 %copy-start.2 = (f32[64]{0:T(128)S(1)}, f32[64]{0:T(128)}, u32[]{:S(2)}) copy-start(f32[64]{0:T(128)} %error_ref.1) | copy-start | bytes 772
  35.6 24.8 %all-to-all-start.1 = ((f32[16,8,2560]{2,1,0:T(8,128)}), f32[16,8,2560]{2,1,0:T(8,128)S(1)}, u32[]{:S(2)}, u32[]{:S(2)}) async-start(f32[16,8,2560]{2,1,0:T(8,128)} %get-tuple-element.8), calls=%async_computation.1 | async-start | bytes 2621440 | tf_op jit(solution)/shard_map/all_to_all | solution.py:220

commit v2 on v1

--- a/solution.py
+++ b/solution.py
@@ -28,18 +28,44 @@
     return pltpu.CompilerParams(vmem_limit_bytes=40 << 20, **more)
 
 
-def split_kernel(where_ref, mine_ref, block_ref, whole_ref, packed_ref, sent_ref, tiles, sems):
-    step = pl.program_id(0)
+def gather_kernel(holder_ref, column_ref, whole_ref, out_ref, tiles, sems):
+    region = lax.axis_index("region")
 
     def fetch(k):
-        start = pl.multiple_of((where_ref[k] // 128) * 128, 128)
+        start = lax.bitwise_and(holder_ref[k], COLS - 1) * S_DEV + lax.bitwise_and(column_ref[k], -128)
+        start = pl.multiple_of(start, 128)
         return pltpu.make_async_copy(whole_ref.at[:, pl.ds(start, 128)], tiles.at[k], sems.at[k])
 
-    @pl.when(step == 0)
-    def _():
-        for k in range(NOBS):
-            fetch(k).start()
-
+    for k in range(NOBS):
+        fetch(k).start()
+    for k in range(NOBS):
+        fetch(k).wait()
+    lane = lax.broadcasted_iota(jnp.int32, (OWN, 128), 1)
+    got = jnp.zeros((OWN, 128), jnp.float32)
+    for k in range(NOBS):
+        turned = pltpu.roll(tiles[k], lax.bitwise_and(k - column_ref[k], 127), 1)
+        home = lax.shift_right_logical(holder_ref[k], 4)
+        got = jnp.where(lane == jnp.where(home == region, k, -1), turned, got)
+    full = jnp.concatenate([got, jnp.zeros((8 - OWN, 128), jnp.float32)], axis=0)
+    out_ref[...] = jnp.broadcast_to(full[None], out_ref.shape)
+
+
+def gather(holder, column, ensemble):
+    return pl.pallas_call(
+        gather_kernel,
+        in_specs=[SMEM, SMEM, pl.BlockSpec(memory_space=pltpu.HBM)],
+        out_specs=VMEM,
+        out_shape=jax.ShapeDtypeStruct((REGIONS, 8, 128), jnp.float32),
+        scratch_shapes=[
+            pltpu.VMEM((NOBS, OWN, 128), jnp.float32),
+            pltpu.SemaphoreType.DMA((NOBS,)),
+        ],
+        compiler_params=params(),
+        name="gather",
+    )(holder, column, ensemble)
+
+
+def pack_kernel(block_ref, packed_ref):
     for b in range(GROUP):
         low = b * S_DEV
         packed_ref[b, 0:OWN, :] = block_ref[:, low : low + HEAD]
@@ -50,43 +76,37 @@
                     q : q + 1, at : at + PIECE
                 ]
 
-    @pl.when(step == pl.num_programs(0) - 1)
-    def _():
-        lane = lax.broadcasted_iota(jnp.int32, (OWN, 128), 1)
-        got = jnp.zeros((OWN, 128), jnp.float32)
-        for k in range(NOBS):
-            fetch(k).wait()
-            turned = pltpu.roll(tiles[k], lax.rem(k + 128 - lax.rem(where_ref[k], 128), 128), 1)
-            got = jnp.where(lane == jnp.where(mine_ref[k] == 1, k, -1), turned, got)
-        full = jnp.concatenate([got, jnp.zeros((8 - OWN, 128), jnp.float32)], axis=0)
-        sent_ref[...] = jnp.broadcast_to(full[None], sent_ref.shape)
-
-
-def split(where, mine, ensemble):
-    return pl.pallas_call(
-        split_kernel,
+
+def pack(ensemble):
+    return pl.pallas_call(
+        pack_kernel,
         grid=(COLS // GROUP,),
-        in_specs=[
-            SMEM,
-            SMEM,
-            pl.BlockSpec((OWN, GROUP * S_DEV), lambda s: (0, s)),
-            pl.BlockSpec(memory_space=pl.ANY),
-        ],
-        out_specs=[
-            pl.BlockSpec((GROUP, 8, HEAD), lambda s: (s, 0, 0)),
-            pl.BlockSpec((REGIONS * COLS, 8, 128), lambda s: (0, 0, 0)),
-        ],
-        out_shape=[
-            jax.ShapeDtypeStruct((COLS, 8, HEAD), jnp.float32),
-            jax.ShapeDtypeStruct((REGIONS * COLS, 8, 128), jnp.float32),
-        ],
-        scratch_shapes=[
-            pltpu.VMEM((NOBS, OWN, 128), jnp.float32),
-            pltpu.SemaphoreType.DMA((NOBS,)),
-        ],
-        compiler_params=params(),
-        name="split",
-    )(where, mine, ensemble, ensemble)
+        in_specs=[pl.BlockSpec((OWN, GROUP * S_DEV), lambda s: (0, s))],
+        out_specs=pl.BlockSpec((GROUP, 8, HEAD), lambda s: (s, 0, 0)),
+        out_shape=jax.ShapeDtypeStruct((COLS, 8, HEAD + 128), jnp.float32),
+        compiler_params=params(),
+        name="pack",
+    )(ensemble)
+
+
+def place_kernel(got_ref, packed_ref, out_ref, copies, sem):
+    copies[...] = jnp.broadcast_to(jnp.sum(got_ref[...], axis=0)[None], copies.shape)
+    move = pltpu.make_async_copy(copies, out_ref.at[:, :, pl.ds(HEAD, 128)], sem)
+    move.start()
+    move.wait()
+
+
+def place(got, packed):
+    return pl.pallas_call(
+        place_kernel,
+        in_specs=[VMEM, pl.BlockSpec(memory_space=pl.ANY)],
+        out_specs=pl.BlockSpec(memory_space=pl.ANY),
+        out_shape=jax.ShapeDtypeStruct(packed.shape, jnp.float32),
+        input_output_aliases={1: 0},
+        scratch_shapes=[pltpu.VMEM((COLS, 8, 128), jnp.float32), pltpu.SemaphoreType.DMA],
+        compiler_params=params(),
+        name="place",
+    )(got, packed)
 
 
 def total(x):
@@ -94,11 +114,8 @@
 
 
 def chain_kernel(value_ref, error_ref, own_ref, got_ref, weight_ref, out_ref, scratch):
-    gathered = got_ref[0:COLS]
-    for r in range(1, REGIONS):
-        gathered = gathered + got_ref[r * COLS : (r + 1) * COLS]
     for c in range(COLS):
-        scratch[OWN * c : OWN * (c + 1), :] = gathered[c, 0:OWN, :]
+        scratch[OWN * c : OWN * (c + 1), :] = got_ref[c, 0:OWN, :]
     priors = scratch[...]
     mean = total(priors) * (1.0 / MEMBERS)
     spread = priors - mean
@@ -137,12 +154,12 @@
 def chain(value, error, own, got, weight):
     return pl.pallas_call(
         chain_kernel,
-        in_specs=[SMEM, SMEM, SMEM, VMEM, VMEM],
+        grid=(1,),
+        in_specs=[SMEM, SMEM, SMEM, pl.BlockSpec((COLS, 8, 128), lambda s: (0, 0, HEAD // 128)), VMEM],
         out_specs=VMEM,
         out_shape=jax.ShapeDtypeStruct((PADDED, 128), jnp.float32),
         scratch_shapes=[pltpu.VMEM((MEMBERS, 128), jnp.float32)],
         compiler_params=params(),
-        cost_estimate=pl.CostEstimate(flops=20_000_000, bytes_accessed=20_000_000, transcendentals=0),
         name="chain",
     )(value, error, own, got, weight)
 
@@ -209,17 +226,16 @@
     region = lax.axis_index("region")
     weight = loc_mask.astype(jnp.float32) * loc_taper
     home = observation_holder // COLS
-    mine = (home == region).astype(jnp.int32)
-    where = (observation_holder - home * COLS) * S_DEV + obs_column
     mutual = jnp.zeros((NOBS, NOBS), jnp.float32)
     for r in range(REGIONS):
         mutual = jnp.where(home[None, :] == r, weight[:, r : r + 1], mutual)
     mutual = jnp.pad(mutual, ((0, 0), (0, 128 - NOBS)))
     own = lax.dynamic_index_in_dim(weight, region, 1, keepdims=False)
-    packed, sent = split(where, mine, ensemble)
-    state = lax.all_to_all(packed, "cols", 0, 0)
-    got = lax.all_to_all(sent, ("region", "cols"), 0, 0)
-    turn = chain(obs_value, obs_error, own, got, mutual)
+    priors = gather(observation_holder, obs_column, ensemble)
+    packed = pack(ensemble)
+    priors = lax.all_to_all(priors, "region", 0, 0)
+    state = lax.all_to_all(place(priors, packed), "cols", 0, 0)
+    turn = chain(obs_value, obs_error, own, state, mutual)
     state = apply(turn, state)
     state = lax.all_to_all(state, "cols", 0, 0)
     return join(state)

time: 86.4 us -> 75.8 us (0.88)
  blocking collectives: 46.4 us -> 21.3 us
  waiting for transfers between devices: 16 us -> 25 us
  starting transfers between devices: 3.85 us -> 12.6 us
  Pallas kernels: 16.7 us -> 13.3 us
  local copies, waits for them, and re-layouts: 1.62 us -> 2.96 us
  other arithmetic: 1.49 us -> 0.16 us
    all_to_all x1 -> x0, blocking collectives: 24.6 us -> none  [per_device(): got = lax.all_to_all(sent, ('region', 'cols'), 0, 0)]
    all_to_all x1 -> x2, waiting for transfers between devices: 16 us -> 25 us  [the longest x1 21.2 us: per_device(): state = lax.all_to_all(place(priors, packed), 'cols', 0, 0)]
    all_to_all x1 -> x2, starting transfers between devices: 3.85 us -> 12.6 us  [the longest x1 8.19 us: per_device(): state = lax.all_to_all(place(priors, packed), 'cols', 0, 0)]
    pallas_call x2 -> x4, Pallas kernels: 12.8 us -> 9.47 us  [the longest x1 4.68 us: chain(): pl.pallas_call(chain_kernel, grid=(1,), in_specs=[SMEM, SMEM, SMEM, pl.Bl...]
    unnamed x10 -> x18, local copies, waits for them, and re-layouts: 1.6 us -> 2.94 us
  transfers between devices with their start and end apart: 1 -> 2, of which waited for: 1 -> 2; matrix products, arithmetic and copies ran while one was open for 0% -> 0% of each run, Pallas kernels for 5% -> 2%
where the time goes in v2:
time: 75.8 us; the launch traced here: 75.4 us
  waiting for transfers between devices  25 us (33%)
  blocking collectives  21.3 us (28%)
  Pallas kernels  13.3 us (18%)
  starting transfers between devices  12.6 us (17%)
  local copies, waits for them, and re-layouts  2.96 us (4%)
    all_to_all x1, blocking collectives, per_device(): state = lax.all_to_all(state, 'cols', 0, 0)  21.3 us
    all_to_all x1, waiting for transfers between devices, per_device(): state = lax.all_to_all(place(priors, packed), 'cols', 0, 0)  21.2 us
    all_to_all x1, starting transfers between devices, per_device(): state = lax.all_to_all(place(priors, packed), 'cols', 0, 0)  8.19 us
    pallas_call x1, Pallas kernels, chain(): pl.pallas_call(chain_kernel, grid=(1,), in_specs=[SMEM, SMEM, SMEM, pl.Bl...  4.68 us
    all_to_all x1, starting transfers between devices, per_device(): priors = lax.all_to_all(priors, 'region', 0, 0)  4.4 us
    all_to_all x1, waiting for transfers between devices, per_device(): priors = lax.all_to_all(priors, 'region', 0, 0)  3.74 us
    unnamed x18, local copies, waits for them, and re-layouts  2.94 us
    pallas_call x1, Pallas kernels, gather(): pl.pallas_call(gather_kernel, in_specs=[SMEM, SMEM, pl.BlockSpec(memory_s...  2.43 us
  transfers between devices with their start and end apart: 2, of which 2 were waited for; matrix products, arithmetic and copies ran while one was open for 0% of the time, Pallas kernels for 2%

profile of v2, /device:TPU:0, one launch (start us, length us, event | category | flops | bytes accessed | tf_op | source)
XLA Modules:
  0.0 75.4 jit_solution(13354373956050613809)
XLA Ops:
  0.0 1.6 %copy-done = f32[5,65536]{1,0:T(8,128)S(1)} copy-done((f32[5,65536]{1,0:T(8,128)S(1)}, f32[5,65536]{1,0:T(8,128)}, u32[]{:S(2)}) %copy-start) | copy-done | bytes 1310744
  1.6 0.7 copy-done.4
  2.2 0.7 copy-done.5
  2.9 2.4 %gather.1 = f32[8,8,128]{2,1,0:T(8,128)} custom-call(s32[64]{0:T(128)S(1)} %copy-done.5, s32[64]{0:T(128)S(1)} %copy-done.4, f32[5,65536]{1,0:T(8,128)S(1)} %copy-done), custom_call_target="tpu_custom_call" | custom-call | tf_op jit(solution)/shard_map/gather/pallas_call | solution.py:54
  5.3 4.4 %all-to-all-start = ((f32[8,8,128]{2,1,0:T(8,128)}), f32[8,8,128]{2,1,0:T(8,128)S(1)}, u32[]{:S(2)}, u32[]{:S(2)}) async-start(f32[8,8,128]{2,1,0:T(8,128)} %gather.1), calls=%async_computation | async-start | bytes 65536 | tf_op jit(solution)/shard_map/all_to_all | solution.py:236
  9.7 0.0 copy-done.1
  9.7 1.7 %pack.1.packed_ref = f32[16,8,2688]{2,1,0:T(8,128)} custom-call(f32[5,65536]{1,0:T(8,128)S(1)} %copy-done.1), custom_call_target="tpu_custom_call" | custom-call | tf_op jit(solution)/shard_map/pack/pallas_call | solution.py:81
  11.5 3.7 %all-to-all-done.got_ref = f32[8,8,128]{2,1,0:T(8,128)S(1)} async-done(((f32[8,8,128]{2,1,0:T(8,128)}), f32[8,8,128]{2,1,0:T(8,128)S(1)}, u32[]{:S(2)}, u32[]{:S(2)}) %all-to-all-start) | async-done | bytes 32800 | tf_op jit(solution)/shard_map/all_to_all | solution.py:236
  15.2 0.6 place.1
  15.8 0.0 copy-start.6
  15.9 0.0 copy-start.7
  15.9 0.0 copy-start.8
  15.9 0.0 copy-start.2
  15.9 0.0 copy-start.3
  15.9 8.2 %all-to-all-start.1 = ((f32[16,8,2688]{2,1,0:T(8,128)}), f32[16,8,2688]{2,1,0:T(8,128)S(1)}, u32[]{:S(2)}, u32[]{:S(2)}) async-start(f32[16,8,2688]{2,1,0:T(8,128)} %place.1), calls=%async_computation.1 | async-start | bytes 2752512 | tf_op jit(solution)/shard_map/all_to_all | solution.py:237
  24.1 0.0 copy-done.6
  24.2 0.0 copy-done.7
  24.2 0.0 copy-done.8
  24.2 0.1 select_select_fusion
  24.4 21.2 %all-to-all-done.1.got_ref = f32[16,8,2688]{2,1,0:T(8,128)S(1)} async-done(((f32[16,8,2688]{2,1,0:T(8,128)}), f32[16,8,2688]{2,1,0:T(8,128)S(1)}, u32[]{:S(2)}, u32[]{:S(2)}) %all-to-all-start.1) | async-done | bytes 1376288 | tf_op jit(solution)/shard_map/all_to_all | solution.py:237
  45.6 4.7 %chain.1.turn_ref = f32[128,128]{1,0:T(8,128)S(1)} custom-call(f32[64]{0:T(128)S(1)} %copy-done.2, f32[64]{0:T(128)S(1)} %copy-done.3, f32[64]{0:T(128)S(1)} %get-tuple-element.15.own_ref, f32[16,8,2688]{2,1,0:T(8,128)S(1)} %all-to-all-done.1.got_ref, f32[64,128]{1,0:T(8,128)S(1)} %pad.4.weight_ref), custom_call_target="tpu_custom_call" | custom-call | tf_op jit(solution)/shard_map/chain/pallas_call | solution.py:155
  50.3 2.0 %apply.1 = f32[16,8,2560]{2,1,0:T(8,128)S(1)} custom-call(f32[128,128]{1,0:T(8,128)S(1)} %chain.1.turn_ref, f32[16,8,2688]{2,1,0:T(8,128)S(1)} %all-to-all-done.1.got_ref), custom_call_target="tpu_custom_call" | custom-call | tf_op jit(solution)/shard_map/apply/pallas_call | solution.py:190
  52.3 21.3 %all_to_all.15.packed_ref = f32[16,8,2560]{2,1,0:T(8,128)S(1)} all-to-all(f32[16,8,2560]{2,1,0:T(8,128)S(1)} %apply.1), channel_id=1, replica_groups=mesh['region'=8,'cols'=16] {'cols'}, dimensions={0} | all-to-all | bytes 2621440 | tf_op jit(solution)/shard_map/all_to_all | solution.py:240
  73.5 1.9 %join.1 = f32[5,65536]{1,0:T(8,128)} custom-call(f32[16,8,2560]{2,1,0:T(8,128)S(1)} %all_to_all.15.packed_ref), custom_call_target="tpu_custom_call" | custom-call | tf_op jit(solution)/shard_map/join/pallas_call | solution.py:214
  (11 shorter events, 0.1 us)
Async XLA Ops:
  0.0 1.6 %copy-start = (f32[5,65536]{1,0:T(8,128)S(1)}, f32[5,65536]{1,0:T(8,128)}, u32[]{:S(2)}) copy-start(f32[5,65536]{1,0:T(8,128)} %block_ref.1) | copy-start | bytes 3932164
  1.6 0.7 copy-start.4
  2.2 0.7 copy-start.5
  2.9 6.8 %copy-start.1 = (f32[5,65536]{1,0:T(8,128)S(1)}, f32[5,65536]{1,0:T(8,128)}, u32[]{:S(2)}) copy-start(f32[5,65536]{1,0:T(8,128)} %block_ref.1) | copy-start | bytes 3932164
  5.3 9.8 %all-to-all-start = ((f32[8,8,128]{2,1,0:T(8,128)}), f32[8,8,128]{2,1,0:T(8,128)S(1)}, u32[]{:S(2)}, u32[]{:S(2)}) async-start(f32[8,8,128]{2,1,0:T(8,128)} %gather.1), calls=%async_computation | async-start | bytes 65536 | tf_op jit(solution)/shard_map/all_to_all | solution.py:236
  15.8 8.3 %copy-start.6 = (s32[64]{0:T(128)S(1)}, s32[64]{0:T(128)}, u32[]{:S(2)}) copy-start(s32[64]{0:T(128)} %holder_ref.1) | copy-start | bytes 772
  15.9 8.3 %copy-start.7 = (f32[64,8]{0,1:T(8,128)S(1)}, f32[64,8]{0,1:T(8,128)}, u32[]{:S(2)}) copy-start(f32[64,8]{0,1:T(8,128)} %param.13) | copy-start | bytes 6148
  15.9 8.3 %copy-start.8 = (s32[64,8]{0,1:T(8,128)S(1)}, s32[64,8]{0,1:T(8,128)}, u32[]{:S(2)}) copy-start(s32[64,8]{0,1:T(8,128)} %param.12) | copy-start | bytes 6148
  15.9 29.7 %copy-start.2 = (f32[64]{0:T(128)S(1)}, f32[64]{0:T(128)}, u32[]{:S(2)}) copy-start(f32[64]{0:T(128)} %value_ref.1) | copy-start | bytes 772
  15.9 29.7 %copy-start.3 = (f32[64]{0:T(128)S(1)}, f32[64]{0:T(128)}, u32[]{:S(2)}) copy-start(f32[64]{0:T(128)} %error_ref.1) | copy-start | bytes 772
  15.9 29.7 %all-to-all-start.1 = ((f32[16,8,2688]{2,1,0:T(8,128)}), f32[16,8,2688]{2,1,0:T(8,128)S(1)}, u32[]{:S(2)}, u32[]{:S(2)}) async-start(f32[16,8,2688]{2,1,0:T(8,128)} %place.1), calls=%async_computation.1 | async-start | bytes 2752512 | tf_op jit(solution)/shard_map/all_to_all | solution.py:237

commit v3 on v0

v3 whole, which is shorter than its diff:
```python
import jax
import jax.numpy as jnp
from jax import lax
from jax.experimental import pallas as pl
from jax.experimental.pallas import tpu as pltpu
from jax.sharding import PartitionSpec as P

MEMBERS = 80
NOBS = 64
COLS = 16
REGIONS = 8
OWN = 5
S_DEV = 4096
REGION_COLUMNS = COLS * S_DEV
HALF = S_DEV // 2
PIECE = S_DEV // 8
FULL = HALF + PIECE
PADDED = COLS * 8
BLOCK = 4
SPARE = MEMBERS - 1

SMEM = pl.BlockSpec(memory_space=pltpu.SMEM)
VMEM = pl.BlockSpec(memory_space=pltpu.VMEM)
HBM = pl.BlockSpec(memory_space=pltpu.HBM)


def params(size=40 << 20):
    return pltpu.CompilerParams(vmem_limit_bytes=size)


def split_kernel(
    holder_ref, column_ref, whole_ref, row_ref, mask_ref, taper_ref, packed_ref, out_ref, weight_ref,
    held, holders, columns, row, mask, taper, sems, small_sems
):
    region = lax.axis_index("region")
    small = [(holder_ref, holders), (column_ref, columns), (row_ref, row), (mask_ref, mask), (taper_ref, taper)]
    small = [pltpu.make_async_copy(a, b, small_sems.at[n]) for n, (a, b) in enumerate(small)]

    def fetch(b):
        part = pl.ds(b * S_DEV, S_DEV)
        return pltpu.make_async_copy(whole_ref.at[:, part], held.at[:, part], sems.at[b])

    for copy in small:
        copy.start()
    for b in range(COLS):
        fetch(b).start()
    for copy in small:
        copy.wait()
    weight = (mask[...].astype(jnp.float32) * taper[...]).T
    home = lax.shift_right_logical(row[...], 4)
    mutual = jnp.zeros((NOBS, NOBS), jnp.float32)
    own = jnp.zeros((NOBS, 128), jnp.float32)
    for r in range(REGIONS):
        column = weight[:, r : r + 1]
        mutual = jnp.where(home == r, jnp.broadcast_to(column, (NOBS, NOBS)), mutual)
        own = jnp.where(region == r, jnp.broadcast_to(column, (NOBS, 128)), own)
    weight_ref[0] = jnp.concatenate([mutual, jnp.zeros((NOBS, 128 - NOBS), jnp.float32)], axis=1)
    weight_ref[1] = own
    for b in range(COLS):
        fetch(b).wait()
        low = b * S_DEV
        first = held[0:4, low : low + HALF]
        second = held[0:4, low + HALF : low + S_DEV]
        packed_ref[b, :, 0:HALF] = jnp.concatenate([first, second], axis=0)
        last = [held[4:5, low + s * PIECE : low + (s + 1) * PIECE] for s in range(8)]
        packed_ref[b, :, HALF:FULL] = jnp.concatenate(last, axis=0)
    lane = lax.broadcasted_iota(jnp.int32, (OWN, 128), 1)
    got = jnp.zeros((OWN, 128), jnp.float32)
    for k in range(NOBS):
        holder, column = holders[k], columns[k]
        start = lax.bitwise_and(holder, COLS - 1) * S_DEV + lax.bitwise_and(column, S_DEV - 128)
        tile = held[:, pl.ds(pl.multiple_of(start, 128), 128)]
        turned = pltpu.roll(tile, lax.bitwise_and(k - column, 127), 1)
        at = jnp.where(lax.shift_right_logical(holder, 4) == region, k, -1)
        got = jnp.where(lane == at, turned, got)
    full = jnp.concatenate([got, jnp.zeros((8 - OWN, 128), jnp.float32)], axis=0)
    out_ref[...] = jnp.broadcast_to(full[None], out_ref.shape)


def split(*inputs):
    return pl.pallas_call(
        split_kernel,
        in_specs=[HBM] * 6,
        out_specs=[VMEM] * 3,
        out_shape=[
            pltpu.VMEM((COLS, 8, FULL + 128), jnp.float32),
            pltpu.VMEM((REGIONS, 8, 128), jnp.float32),
            pltpu.VMEM((2, NOBS, 128), jnp.float32),
        ],
        scratch_shapes=[
            pltpu.VMEM((OWN, REGION_COLUMNS), jnp.float32),
            pltpu.SMEM((NOBS,), jnp.int32),
            pltpu.SMEM((NOBS,), jnp.int32),
            pltpu.VMEM((1, NOBS), jnp.int32),
            pltpu.VMEM((REGIONS, NOBS), jnp.int32),
            pltpu.VMEM((REGIONS, NOBS), jnp.float32),
            pltpu.SemaphoreType.DMA((COLS,)),
            pltpu.SemaphoreType.DMA((5,)),
        ],
        compiler_params=params(),
        name="split",
    )(*[pltpu.with_memory_space_constraint(x, pltpu.HBM) for x in inputs])


def place_kernel(got_ref, packed_ref, out_ref, copies, sem):
    copies[...] = jnp.broadcast_to(jnp.sum(got_ref[...], axis=0)[None], copies.shape)
    move = pltpu.make_async_copy(copies, out_ref.at[:, :, pl.ds(FULL, 128)], sem)
    move.start()
    move.wait()


def place(got, packed):
    return pl.pallas_call(
        place_kernel,
        in_specs=[VMEM, pl.BlockSpec(memory_space=pl.ANY)],
        out_specs=pl.BlockSpec(memory_space=pl.ANY),
        out_shape=jax.ShapeDtypeStruct(packed.shape, jnp.float32),
        input_output_aliases={1: 0},
        scratch_shapes=[pltpu.VMEM((COLS, 8, 128), jnp.float32), pltpu.SemaphoreType.DMA],
        compiler_params=params(),
        name="place",
    )(got, packed)


def total(x):
    return jnp.sum(x, axis=0, keepdims=True)


def spread_out(x, shape):
    return jnp.broadcast_to(x, shape)


def chain(value_ref, error_ref, got_ref, weight_ref, scratch, aside):
    for c in range(COLS):
        scratch[OWN * c : OWN * (c + 1), :] = got_ref[c, 0:OWN, FULL : FULL + 128]
    priors = scratch[...]
    mean = total(priors) * (1.0 / MEMBERS)
    spread = priors - mean
    row = lax.broadcasted_iota(jnp.int32, (MEMBERS, 128), 0)
    lane = lax.broadcasted_iota(jnp.int32, (MEMBERS, 128), 1)
    turn = ((row // OWN) * 8 + lax.rem(row, OWN) == lane).astype(jnp.float32)
    lift = jnp.zeros((1, 128), jnp.float32)
    for low in range(0, NOBS, BLOCK):
        near = range(BLOCK)
        p, m, w, dots, d0, d1, c0, c1 = {}, {}, {}, {}, {}, {}, {}, {}
        for j in near:
            p[j] = jnp.broadcast_to(spread[:, low + j : low + j + 1], (MEMBERS, 128))
            m[j] = jnp.broadcast_to(mean[:, low + j : low + j + 1], (1, 128))
            for k in range(j + 1, BLOCK):
                at = weight_ref[0, low + j : low + j + 1, low + k : low + k + 1]
                w[j, k] = jnp.broadcast_to(at, (1, 128))
        for j in near:
            for k in range(j, BLOCK):
                dots[j, k] = total(p[j] * p[k])
            d0[j] = total(p[j] * spread)
            d1[j] = total(p[j] * turn)
        aside(low // BLOCK)
        for j in near:
            e = error_ref[low + j]
            own = dots[j, j]
            s = own * (1.0 / SPARE) + e
            root = jnp.sqrt(jnp.full((1, 128), e, jnp.float32))
            damped = 1.0 / (SPARE * (s + root * (s * lax.rsqrt(s))))
            move = (value_ref[low + j] - m[j]) * (1.0 / (SPARE * s))
            f0 = weight_ref[0, low + j : low + j + 1, :] * d0[j]
            f1 = weight_ref[1, low + j : low + j + 1, :] * d1[j]
            c0[j] = f0 * damped
            c1[j] = f1 * damped
            mean = mean + move * f0
            lift = lift + move * f1
            a = {}
            for k in range(j + 1, BLOCK):
                f = w[j, k] * dots[j, k]
                a[k] = f * damped
                m[k] = m[k] + move * f
            for k in range(j + 1, BLOCK):
                t = dots[j, k] - a[k] * own
                for l in range(k, BLOCK):
                    dots[k, l] = dots[k, l] - a[k] * dots[j, l] - a[l] * t
                d0[k] = d0[k] - a[k] * d0[j] - t * c0[j]
                d1[k] = d1[k] - a[k] * d1[j] - t * c1[j]
                p[k] = p[k] - a[k] * p[j]
        for j in near:
            spread = spread - p[j] * c0[j]
            turn = turn - p[j] * c1[j]
    return turn + lift


def halves(x):
    high = x.astype(jnp.bfloat16)
    return high, (x - high.astype(jnp.float32)).astype(jnp.bfloat16)


def turn_lanes(x):
    lane = lax.rem(lax.broadcasted_iota(jnp.int32, x.shape, 1), 8)
    return jnp.where(lane < 4, pltpu.roll(x, x.shape[1] - 4, 1), pltpu.roll(x, 4, 1))


def apply_kernel(value_ref, error_ref, got_ref, weight_ref, out_ref, scratch, wide, parts):
    row = lax.broadcasted_iota(jnp.int32, (8, PIECE), 0)

    def span(s):
        return slice((s % 4) * PIECE, (s % 4 + 1) * PIECE)

    def unpack(s):
        for c in range(COLS):
            last = got_ref[c, :, HALF:FULL]
            to = 4 if s < 4 else 0
            last = pltpu.roll(last, (to - s) % 8, 0) if (to - s) % 8 else last
            x = jnp.where(row == to, last, got_ref[c, :, span(s)])
            parts[s, 8 * c : 8 * (c + 1), :] = x
        high, low = halves(parts[s])
        wide[s, 0:PADDED, :] = high
        wide[s, PADDED : 2 * PADDED, :] = low

    def aside(n):
        if n % 2 == 0:
            unpack(n // 2)

    turn = chain(value_ref, error_ref, got_ref, weight_ref, scratch, aside)
    square = jnp.zeros((PADDED, 128), jnp.float32)
    rows = []
    for c in range(COLS):
        rows += [turn[OWN * c : OWN * (c + 1), :], jnp.zeros((8 - OWN, 128), jnp.float32)]
    square = jnp.concatenate(rows, axis=0)
    turned = turn_lanes(square)
    for n, q in enumerate((square, turned)):
        high, low = halves(q)
        twice = jnp.concatenate([high, high], axis=1)
        for s in range(4 * n, 4 * n + 4):
            y = jnp.dot(twice, wide[s], preferred_element_type=jnp.float32)
            y = y + jnp.dot(low, wide[s, 0:PADDED, :], preferred_element_type=jnp.float32)
            y = y.reshape(COLS, 8, PIECE)
            if n == 0:
                out_ref[:, 0:4, span(s)] = y[:, 0:4]
            else:
                out_ref[:, 4:8, span(s)] = y[:, 0:4]
            out_ref[:, s : s + 1, HALF:FULL] = y[:, 4:5]


def apply(value, error, got, weight):
    return pl.pallas_call(
        apply_kernel,
        in_specs=[SMEM, SMEM, VMEM, VMEM],
        out_specs=VMEM,
        out_shape=jax.ShapeDtypeStruct((COLS, 8, FULL), jnp.float32),
        scratch_shapes=[
            pltpu.VMEM((MEMBERS, 128), jnp.float32),
            pltpu.VMEM((8, 2 * PADDED, PIECE), jnp.bfloat16),
            pltpu.VMEM((8, PADDED, PIECE), jnp.float32),
        ],
        compiler_params=params(),
        name="apply",
    )(value, error, got, weight)


def join_kernel(packed_ref, out_ref, held, sems):
    def send(b):
        part = pl.ds(b * S_DEV, S_DEV)
        return pltpu.make_async_copy(held.at[:, part], out_ref.at[:, part], sems.at[b])

    for b in range(COLS):
        low = b * S_DEV
        for s in range(8):
            at = (s % 4) * PIECE
            first = packed_ref[b, 0:4, at : at + PIECE]
            if s >= 4:
                first = packed_ref[b, 4:8, at : at + PIECE]
            last = packed_ref[b, s : s + 1, HALF:FULL]
            at = low + s * PIECE
            held[:, at : at + PIECE] = jnp.concatenate([first, last], axis=0)
        send(b).start()
    for b in range(COLS):
        send(b).wait()


def join(packed):
    return pl.pallas_call(
        join_kernel,
        in_specs=[VMEM],
        out_specs=pl.BlockSpec(memory_space=pl.ANY),
        out_shape=jax.ShapeDtypeStruct((OWN, REGION_COLUMNS), jnp.float32),
        scratch_shapes=[
            pltpu.VMEM((OWN, REGION_COLUMNS), jnp.float32),
            pltpu.SemaphoreType.DMA((COLS,)),
        ],
        compiler_params=params(),
        name="join",
    )(packed)


def per_device(ensemble, obs_value, obs_error, observation_holder, obs_column, loc_mask, loc_taper):
    row = observation_holder.reshape(1, NOBS)
    packed, priors, weight = split(
        observation_holder, obs_column, ensemble, row, loc_mask.T, loc_taper.T
    )
    priors = lax.all_to_all(priors, "region", 0, 0)
    state = lax.all_to_all(place(priors, packed), "cols", 0, 0)
    state = apply(obs_value, obs_error, state, weight)
    state = lax.all_to_all(state, "cols", 0, 0)
    return join(state)


def solution(mesh):
    placed = (P("cols", "region"), P(), P(), P(), P(), P(), P())
    return jax.shard_map(
        per_device, mesh=mesh, in_specs=placed, out_specs=P("cols", "region"), check_vma=False
    )
```

time: 790 us -> 68.8 us (0.09)
  blocking collectives: 286 us -> 59.9 us
  loops' own time: 215 us -> 0 us
  local copies, waits for them, and re-layouts: 115 us -> 0.01 us
  other arithmetic: 104 us -> 0 us
  waiting for transfers between devices: 29.2 us -> 0 us
  matrix products: 28.3 us -> 0 us
  Pallas kernels: 0 us -> 8.66 us
  starting transfers between devices: 8.29 us -> 0 us
    psum x4 -> x0, blocking collectives: 254 us -> none  [per_device(): lax.psum(jnp.take(state, columns, axis=1) * owned[None, :], ('region', 'c...]
    another operation x4 -> x0, loops' own time: 215 us -> none  [run_chain(): return lax.fori_loop(0, count, turn, (block, update_transforms))]
    dynamic_slice x193 -> x0, local copies, waits for them, and re-layouts: 98.9 us -> none  [the longest x64 49.9 us: turn(): obs_error[member_count]]
    reduce_sum x128 -> x0, other arithmetic: 77.9 us -> none  [the longest x64 39.1 us: assimilate(): variance = jnp.sum(spread * spread) / (member_list - 1)]
    all_to_all x1 -> x0, waiting for transfers between devices: 29.2 us -> none  [per_device(): lax.all_to_all(ensemble, 'cols', split_axis=1, concat_axis=0, tiled=True)]
    dot_general x133 -> x0, matrix products: 28.3 us -> none  [the longest x64 17.2 us: assimilate(): jnp.einsum('m,rmn->rn', spread, update_transforms, precision=highest)]
    all_to_all x1 -> x3, blocking collectives: 31.6 us -> 59.9 us  [the longest x1 28.2 us: per_device(): state = lax.all_to_all(place(priors, packed), 'cols', 0, 0)]
    add x128 -> x0, other arithmetic: 18.5 us -> none  [the longest x64 11.4 us: assimilate(): update_transforms + (weight_row * scaling)[:, None, None] * shift[None, :...]
  transfers between devices with their start and end apart: 1 -> 0, of which waited for: 1 -> 0; matrix products, arithmetic and copies ran while one was open for 0% -> 0% of each run, Pallas kernels for 0% -> 0%
where the time goes in v3:
time: 68.8 us; the launch traced here: 68.6 us
  blocking collectives  59.9 us (87%)
  Pallas kernels  8.66 us (13%)
    all_to_all x1, blocking collectives, per_device(): state = lax.all_to_all(place(priors, packed), 'cols', 0, 0)  28.2 us
    all_to_all x1, blocking collectives, per_device(): state = lax.all_to_all(state, 'cols', 0, 0)  22.1 us
    all_to_all x1, blocking collectives, per_device(): priors = lax.all_to_all(priors, 'region', 0, 0)  9.63 us
    pallas_call x1, Pallas kernels, apply(): pl.pallas_call(apply_kernel, in_specs=[SMEM, SMEM, VMEM, VMEM], out_specs...  4.78 us
    pallas_call x1, Pallas kernels, split(): pl.pallas_call(split_kernel, in_specs=[HBM] * 6, out_specs=[VMEM] * 3, ou...  2.39 us
    pallas_call x1, Pallas kernels, join(): pl.pallas_call(join_kernel, in_specs=[VMEM], out_specs=pl.BlockSpec(memor...  1.46 us

profile of v3, /device:TPU:0, one launch (start us, length us, event | category | flops | bytes accessed | tf_op | source)
XLA Modules:
  0.0 68.6 jit_solution(17361536002405807871)
XLA Ops:
  0.0 2.4 %split.1 = (f32[16,8,2688]{2,1,0:T(8,128)S(1)}, f32[8,8,128]{2,1,0:T(8,128)S(1)}, f32[2,64,128]{2,1,0:T(8,128)S(1)}) custom-call(s32[64]{0:T(128)} %holder_ref.1, s32[64]{0:T(128)} %column_ref.1, f32[5,65536]{1,0:T(8,128)} %whole_ref.1, s32[1,64]{1,0:T(1,128)} %bitcast.5, s32[8,64]{1,0:T(8,128)} %bitcast.3, f32[8,64]{1,0:T(8,128)} %bitcast.4), custom_call_target="tpu_custom_call" | custom-call | tf_op jit(solution)/shard_map/split/pallas_call | solution.py:81
  2.4 9.6 %all_to_all.15.got_ref = f32[8,8,128]{2,1,0:T(8,128)S(1)} all-to-all(f32[8,8,128]{2,1,0:T(8,128)S(1)} %get-tuple-element.8), channel_id=1, replica_groups=mesh['region'=8,'cols'=16] {'region'}, dimensions={0} | all-to-all | bytes 65536 | tf_op jit(solution)/shard_map/all_to_all | solution.py:297
  12.1 0.0 copy-start
  12.1 0.0 copy-start.1
  12.1 28.2 %all_to_all.16.got_ref = f32[16,8,2688]{2,1,0:T(8,128)S(1)} all-to-all(f32[16,8,2688]{2,1,0:T(8,128)S(1)} %place.1), channel_id=1, replica_groups=mesh['region'=8,'cols'=16] {'cols'}, dimensions={0} | all-to-all | bytes 2752512 | tf_op jit(solution)/shard_map/all_to_all | solution.py:298
  40.3 0.0 copy-done
  40.3 0.0 copy-done.1
  40.3 4.8 %apply.1 = f32[16,8,2560]{2,1,0:T(8,128)S(1)} custom-call(f32[64]{0:T(128)S(1)} %copy-done, f32[64]{0:T(128)S(1)} %copy-done.1, f32[16,8,2688]{2,1,0:T(8,128)S(1)} %all_to_all.16.got_ref, f32[2,64,128]{2,1,0:T(8,128)S(1)} %get-tuple-element.10.weight_ref), custom_call_target="tpu_custom_call" | custom-call | tf_op jit(solution)/shard_map/apply/pallas_call | solution.py:242
  45.1 22.1 %all_to_all.17.packed_ref = f32[16,8,2560]{2,1,0:T(8,128)S(1)} all-to-all(f32[16,8,2560]{2,1,0:T(8,128)S(1)} %apply.1), channel_id=1, replica_groups=mesh['region'=8,'cols'=16] {'cols'}, dimensions={0} | all-to-all | bytes 2621440 | tf_op jit(solution)/shard_map/all_to_all | solution.py:300
  67.1 1.5 %join.1 = f32[5,65536]{1,0:T(8,128)} custom-call(f32[16,8,2560]{2,1,0:T(8,128)S(1)} %all_to_all.17.packed_ref), custom_call_target="tpu_custom_call" | custom-call | tf_op jit(solution)/shard_map/join/pallas_call | solution.py:278
  (1 shorter events, 0.0 us)
Async XLA Ops:
  12.1 28.2 %copy-start = (f32[64]{0:T(128)S(1)}, f32[64]{0:T(128)}, u32[]{:S(2)}) copy-start(f32[64]{0:T(128)} %value_ref.1) | copy-start | bytes 772
  12.1 28.2 %copy-start.1 = (f32[64]{0:T(128)S(1)}, f32[64]{0:T(128)}, u32[]{:S(2)}) copy-start(f32[64]{0:T(128)} %error_ref.1) | copy-start | bytes 772
